TPU v7x, 32 devices: a whole 2x2x4 slice. The times are simulated.
32 devices in a mesh: grid: 8 (over z, x), cols: 4 (over y, core).
Axes of the slice: x: 2, y: 2, z: 4, core: 2. Of those that a mesh axis runs over, the one named last changes fastest.
Arguments:
- basis: float32 [1024, 3, 16, 1024], P('cols', None, 'grid'), may hold values from -1 to 1
- snapshots: float32 [128, 3, 16, 1024], P('cols', None, 'grid'), may hold values from -60 to 60
- permittivity: float32 [3, 16, 1024], P(None, 'grid'), may hold values from 1 to 10
- labels: int32 [16, 1024], P('grid'), may hold values from 0 to 7
- sigma_table: float32 [8], replicated, may hold values from 0.1 to 10
Outputs:
- new_basis: float32 [128, 3, 16, 1024], P('cols', None, 'grid')
- coefficients: float32 [1024, 128], P('cols')
- cross_terms: float32 [3, 1024, 128], P(None, 'cols')
- block_terms: float32 [3, 128, 128], P(None, 'cols')
All inputs are finite; a program needn't handle non-finite values.
Results may differ from a plain program's by a relative error of at most 0.0003.
Values sent between devices are 32-bit elements; how exact they have to be, the bound alone decides.
A program may use at most 128 MiB of HBM per device.

v0:
```python
import jax
import jax.numpy as jnp
from jax import lax
from jax.sharding import PartitionSpec as P

NY = 32
HIGHEST = lax.Precision.HIGHEST


def padded(shard, sides, width):
    for axis, dim in sides:
        size, length = (lax.axis_size(axis), shard.shape[dim])
        up = [(i, (i + 1) % size) for i in range(size - 1)]
        down = [(j, i) for i, j in up]
        last = lax.slice_in_dim(shard, length - width, length, axis=dim)
        leading = lax.slice_in_dim(shard, 0, width, axis=dim)
        before = lax.ppermute(last, axis, up)
        after = lax.ppermute(leading, axis, down)
        shard = jnp.concatenate([before, shard, after], axis=dim)
    return shard


def cells_dot(left_rows, right_rows):
    left_flat = left_rows.reshape(left_rows.shape[0], -1)
    right_flat = right_rows.reshape(right_rows.shape[0], -1)
    return lax.dot_general(
        left_flat,
        right_flat,
        (((1,), (1,)), ((), ())),
        precision=HIGHEST,
        preferred_element_type=jnp.float32,
    )


def combine_rows(weights, fields):
    flattened = fields.reshape(fields.shape[0], -1)
    output_rows = lax.dot_general(
        weights,
        flattened,
        (((0,), (0,)), ((), ())),
        precision=HIGHEST,
        preferred_element_type=jnp.float32,
    )
    return output_rows.reshape((weights.shape[1],) + fields.shape[1:])


def forward_x(field, row_len):
    padding_cols = jnp.zeros(field.shape[:-1] + (row_len,), field.dtype)
    return jnp.concatenate([field[..., row_len:], padding_cols], axis=-1)


def backward_x(field, row_len):
    padding_cols = jnp.zeros(field.shape[:-1] + (row_len,), field.dtype)
    return jnp.concatenate([padding_cols, field[..., :-row_len]], axis=-1)


def forward_y(field, row_len):
    column_pos = lax.broadcasted_iota(jnp.int32, (field.shape[-1],), 0) % row_len
    padding_cols = jnp.zeros(field.shape[:-1] + (1,), field.dtype)
    shifted = jnp.concatenate([field[..., 1:], padding_cols], axis=-1)
    return jnp.where(column_pos != row_len - 1, shifted, 0.0)


def backward_y(field, row_len):
    column_pos = lax.broadcasted_iota(jnp.int32, (field.shape[-1],), 0) % row_len
    padding_cols = jnp.zeros(field.shape[:-1] + (1,), field.dtype)
    shifted = jnp.concatenate([padding_cols, field[..., :-1]], axis=-1)
    return jnp.where(column_pos != 0, shifted, 0.0)


def curl_curl(extended, row_len):
    field_x = extended[:, 0]
    field_y = extended[:, 1]
    field_z = extended[:, 2]

    def middle(field):
        return field[:, 1:-1]

    def plus_x(field):
        return forward_x(field, row_len) - field

    def minus_x(field):
        return field - backward_x(field, row_len)

    def plus_y(field):
        return forward_y(field, row_len) - field

    def minus_y(field):
        return field - backward_y(field, row_len)

    def second_x(field):
        return forward_x(field, row_len) - 2.0 * field + backward_x(field, row_len)

    def second_y(field):
        return forward_y(field, row_len) - 2.0 * field + backward_y(field, row_len)

    def second_z(field):
        return field[:, 2:] - 2.0 * field[:, 1:-1] + field[:, :-2]

    curl_x = (
        -second_y(middle(field_x))
        - second_z(field_x)
        + minus_y(plus_x(middle(field_y)))
        + plus_x(middle(field_z))
        - plus_x(field_z[:, :-2])
    )
    curl_y = (
        -second_x(middle(field_y))
        - second_z(field_y)
        + minus_x(plus_y(middle(field_x)))
        + plus_y(middle(field_z))
        - plus_y(field_z[:, :-2])
    )
    curl_z = (
        -second_x(middle(field_z))
        - second_y(middle(field_z))
        + minus_x(field_x[:, 2:] - middle(field_x))
        + minus_y(field_y[:, 2:] - middle(field_y))
    )
    return jnp.stack([curl_x, curl_y, curl_z], axis=1)


def lookup_sigma(labels, sigma_table):
    region_ids = jnp.arange(sigma_table.shape[0], dtype=jnp.int32)
    picked = jnp.where(labels[None] == region_ids[:, None, None], sigma_table[:, None, None], 0.0)
    return jnp.sum(picked, axis=0)


def apply_ops(fields, permittivity, conductivity):
    extended = padded(fields, (("grid", 2),), 1)
    curl_term = curl_curl(extended, NY)
    mass_term = permittivity[None] * fields
    loss_term = conductivity[None, None] * fields
    return (curl_term, mass_term, loss_term)


def shards(basis, snapshots, permittivity, labels, sigma_table):
    basis_cols = basis.shape[0]
    snap_cols = snapshots.shape[0]
    total_snap = snap_cols * lax.axis_size("cols")
    unknowns = 3 * snapshots.shape[3] * snapshots.shape[2] * lax.axis_size("grid")
    conductivity = lookup_sigma(labels, sigma_table)
    current = snapshots
    coefficients = jnp.zeros((basis_cols, total_snap), jnp.float32)
    for sweep_index in range(2):
        partial_value = cells_dot(basis, lax.all_gather(current, "cols", axis=0, tiled=True))
        coef_part = lax.psum(partial_value, "grid")
        current = current - lax.psum_scatter(
            combine_rows(coef_part, basis), "cols", scatter_dimension=0, tiled=True
        )
        coefficients = coefficients + coef_part
    finished = lax.all_gather(current, "cols", axis=0, tiled=True)
    own_start = lax.axis_index("cols") * snap_cols
    identity = jnp.eye(total_snap, dtype=jnp.float32)
    gram_sum = lax.psum(cells_dot(finished, finished) / unknowns, "grid")
    lower_factor = jnp.linalg.cholesky(gram_sum)
    inverse = jax.scipy.linalg.solve_triangular(lower_factor, identity, lower=True)
    new_all = combine_rows(inverse.T, finished)
    curl_term, mass_term, loss_term = apply_ops(new_all, permittivity, conductivity)
    own_new = lax.dynamic_slice_in_dim(new_all, own_start, snap_cols, 0)
    cross_part = jnp.stack(
        [cells_dot(basis, curl_term), cells_dot(basis, mass_term), cells_dot(basis, loss_term)],
        axis=0,
    )
    block_part = (
        jnp.stack(
            [
                cells_dot(own_new, curl_term),
                cells_dot(own_new, mass_term),
                cells_dot(own_new, loss_term),
            ],
            axis=0,
        )
        / unknowns
    )
    cross_terms, block_terms = lax.psum((cross_part, block_part), "grid")
    return (own_new, coefficients, cross_terms, block_terms)


def solution(mesh):
    placed = (
        P("cols", None, "grid", None),
        P("cols", None, "grid", None),
        P(None, "grid", None),
        P("grid", None),
        P(),
    )
    return jax.shard_map(
        shards,
        mesh=mesh,
        in_specs=placed,
        out_specs=(
            P("cols", None, "grid", None),
            P("cols", None),
            P(None, "cols", None),
            P(None, "cols", None),
        ),
        check_vma=False,
    )
```

profile of v0, /device:TPU:0, one launch (start us, length us, event | category | flops | bytes accessed | tf_op | source)
XLA Modules:
  0.0 642.6 jit_solution(8649278137576237144)
XLA Ops:
  9.5 31.9 %all-gather.4.cloned.1.call-done = f32[128,3,2,1024]{3,0,2,1:T(8,128)} async-done(((f32[32,3,2,1024]{3,0,2,1:T(8,128)}), f32[128,3,2,1024]{3,0,2,1:T(8,128)}) %all-gather.4.cloned.1.call-update) | async-done | bytes 3145744 | tf_op jit(solution)/shard_map/all_gather | solution.py:146
  41.4 10.8 %fusion.23 = f32[256,128]{1,0:T(8,128)} fusion(f32[128,3,2,1024]{3,0,2,1:T(8,128)} %all-gather.4.cloned.1.call-done, f32[256,3,2,1024]{3,2,1,0:T(2,128)} %param.5), kind=kOutput, calls=%fused_computation.28 | convolution fusion | flops 2415919104 | bytes 9568256 | tf_op jit(solution)/shard_map/dot_general | solution.py:26
  52.2 9.0 %reshape.49 = f32[256,6144]{1,0:T(8,128)} reshape(f32[256,3,2,1024]{3,2,1,0:T(2,128)} %param.5) | data formatting | bytes 12582912 | tf_op jit(solution)/shard_map/reshape | solution.py:24
  61.2 6.6 %copy.42 = f32[6144,256]{1,0:T(8,128)} copy(f32[6144,256]{0,1:T(8,128)} %bitcast.112) | data formatting | bytes 12582912 | tf_op jit(solution)/shard_map/dot_general | solution.py:37
  67.8 54.2 %all-reduce.19.cloned.1.call-done = f32[256,128]{1,0:T(8,128)} async-done(((f32[256,128]{1,0:T(8,128)}), f32[256,128]{1,0:T(8,128)}) %all-reduce.19.cloned.1.call-update) | async-done | bytes 131088 | tf_op jit(solution)/shard_map/psum | solution.py:147
  122.0 11.2 %fusion.63 = f32[128,3,2,1024]{3,0,2,1:T(8,128)} fusion(f32[3,2,1024,256]{3,2,1,0:T(8,128)} %bitcast.110, f32[256,128]{1,0:T(8,128)} %all-reduce.19.cloned.1.call-done), kind=kOutput, calls=%fused_computation.61 | convolution fusion | flops 2415919104 | bytes 9568256 | tf_op jit(solution)/shard_map/dot_general | solution.py:37
  133.6 37.1 %reduce-scatter.3.cloned.1.call-done = f32[32,3,2,1024]{3,0,2,1:T(8,128)} async-done(((f32[128,3,2,1024]{3,0,2,1:T(8,128)}), f32[32,3,2,1024]{3,0,2,1:T(8,128)}) %reduce-scatter.3.cloned.1.call-update) | async-done | bytes 786448 | tf_op jit(solution)/shard_map/reduce_scatter | solution.py:148
  173.1 28.6 %all-gather.6.cloned.1.call-done = f32[128,3,2,1024]{3,0,2,1:T(8,128)} async-done(((f32[32,3,2,1024]{3,0,2,1:T(8,128)}), f32[128,3,2,1024]{3,0,2,1:T(8,128)}) %all-gather.6.cloned.1.call-update) | async-done | bytes 3145744 | tf_op jit(solution)/shard_map/all_gather | solution.py:146
  201.7 10.7 %fusion.26 = f32[256,128]{1,0:T(8,128)} fusion(f32[128,3,2,1024]{3,0,2,1:T(8,128)} %all-gather.6.cloned.1.call-done, f32[256,3,2,1024]{3,2,1,0:T(2,128)} %param.5), kind=kOutput, calls=%fused_computation.29 | convolution fusion | flops 2415919104 | bytes 9568256 | tf_op jit(solution)/shard_map/dot_general | solution.py:26
  212.4 69.8 %all-reduce.21.cloned.1.call-done = f32[256,128]{1,0:T(8,128)} async-done(((f32[256,128]{1,0:T(8,128)}), f32[256,128]{1,0:T(8,128)}) %all-reduce.21.cloned.1.call-update) | async-done | bytes 131088 | tf_op jit(solution)/shard_map/psum | solution.py:147
  282.2 11.2 %fusion.61 = f32[128,3,2,1024]{3,0,2,1:T(8,128)} fusion(f32[3,2,1024,256]{3,2,1,0:T(8,128)} %bitcast.111, f32[256,128]{1,0:T(8,128)} %all-reduce.21.cloned.1.call-done), kind=kOutput, calls=%fused_computation.59 | convolution fusion | flops 2415919104 | bytes 9568256 | tf_op jit(solution)/shard_map/dot_general | solution.py:37
  293.5 37.3 %reduce-scatter.5.cloned.1.call-done = f32[32,3,2,1024]{3,0,2,1:T(8,128)} async-done(((f32[128,3,2,1024]{3,0,2,1:T(8,128)}), f32[32,3,2,1024]{3,0,2,1:T(8,128)}) %reduce-scatter.5.cloned.1.call-update) | async-done | bytes 786448 | tf_op jit(solution)/shard_map/reduce_scatter | solution.py:148
  333.4 28.2 %all-gather.8.cloned.1.call-done = f32[128,3,2,1024]{3,0,2,1:T(8,128)} async-done(((f32[32,3,2,1024]{3,0,2,1:T(8,128)}), f32[128,3,2,1024]{3,0,2,1:T(8,128)}) %all-gather.8.cloned.1.call-update) | async-done | bytes 3145744 | tf_op jit(solution)/shard_map/all_gather | solution.py:152
  361.7 6.3 fusion.42
  370.4 66.2 %all-reduce.23.cloned.1.call-done = f32[128,128]{0,1:T(8,128)} async-done(((f32[128,128]{0,1:T(8,128)}), f32[128,128]{0,1:T(8,128)}) %all-reduce.23.cloned.1.call-update) | async-done | bytes 65552 | tf_op jit(solution)/shard_map/psum | solution.py:155
  438.4 11.7 %cholesky.17 = f32[128,128]{1,0:T(8,128)S(1)} custom-call(f32[128,128]{1,0:T(8,128)S(1)} %fusion.67), custom_call_target="Cholesky" | custom-call | tf_op jit(solution)/shard_map/jit(cholesky)/cholesky | solution.py:156
  451.4 9.8 %custom-call.7 = f32[1,128,128]{1,2,0:T(8,128)S(1)} custom-call(f32[1,128,128]{2,1,0:T(8,128)S(1)} %fusion.65), custom_call_target="InvertDiagBlocksLowerTriangular" | custom-call | tf_op jit(solution)/shard_map/jit(_solve_triangular)/triangular_solve | solution.py:157
  461.5 4.7 fusion.10
  479.0 9.9 %fusion.37 = f32[1,256,128]{1,2,0:T(8,128)S(1)} fusion(f32[256,3,2,1024]{3,2,1,0:T(2,128)} %param.5, f32[128,3,2,1024]{3,0,2,1:T(8,128)S(1)} %fusion.10, f32[2,1024]{1,0:T(2,128)S(1)} %select_reduce_fusion), kind=kOutput, calls=%fused_computation.32 | convolution fusion | flops 2416705536 | bytes 9576448 | tf_op jit(solution)/shard_map/dot_general | solution.py:26
  488.9 7.2 %fusion.32 = f32[1,256,128]{1,2,0:T(8,128)S(1)} fusion(f32[256,3,2,1024]{3,2,1,0:T(2,128)S(1)} %bitcast.109, f32[128,3,2,1024]{3,0,2,1:T(8,128)S(1)} %fusion.10, f32[3,2,1024]{2,1,0:T(2,128)S(1)} %copy-done.15), kind=kOutput, calls=%fused_computation.31 | convolution fusion | flops 2416705536 | bytes 9592832 | tf_op jit(solution)/shard_map/dot_general | solution.py:26
  496.2 41.0 %collective-permute-done = f32[128,3,1,1024]{3,0,2,1:T(8,128)} collective-permute-done((f32[128,3,1,1024]{3,0,2,1:T(8,128)}, f32[128,3,1,1024]{3,0,2,1:T(8,128)}, u32[]{:S(2)}, u32[]{:S(2)}) %collective-permute-start) | collective-permute-done | bytes 1572896 | tf_op jit(solution)/shard_map/ppermute | solution.py:17
  553.0 7.3 %fusion.29 = f32[1,256,128]{1,2,0:T(8,128)S(1)} fusion(f32[256,3,2,1024]{3,2,1,0:T(2,128)S(1)} %bitcast.109, f32[128,1,2,1024]{3,0,2,1:T(8,128)S(1)} %add_bitcast_fusion, f32[128,1,2,1024]{3,0,2,1:T(8,128)S(1)} %fusion.54, f32[128,1,2,1024]{3,0,2,1:T(8,128)S(1)} %get-tuple-element.19), kind=kOutput, calls=%fused_computation.30 | convolution fusion | flops 2417491968 | bytes 9568256 | tf_op jit(solution)/shard_map/dot_general | solution.py:26
  570.3 37.2 %psum.39 = f32[3,32,128]{2,1,0:T(8,128)} all-reduce(f32[3,32,128]{2,1,0:T(8,128)S(1)} %maximum_multiply_fusion), channel_id=1, replica_groups=mesh['grid'=8,'cols'=4] {'grid'}, use_global_device_ids=true, to_apply=%region_9.10 | all-reduce | flops 12288 | bytes 98304 | tf_op jit(solution)/shard_map/psum | solution.py:176
  607.5 26.2 %all-reduce.25.cloned.1.call-done = f32[3,256,128]{1,2,0:T(8,128)} async-done(((f32[3,256,128]{1,2,0:T(8,128)}), f32[3,256,128]{1,2,0:T(8,128)}) %all-reduce.25.cloned.1.call-update) | async-done | bytes 393232 | tf_op jit(solution)/shard_map/psum | solution.py:176
  (92 shorter events, 53.7 us)
Async XLA Ops:
  7.2 34.2 %all-gather.4.cloned.1.call-start = ((), (), s32[]{:S(2)}) async-start(), calls=%async_computation.2 | async-start | bytes 3932160 | tf_op jit(solution)/shard_map/all_gather | solution.py:146
  9.5 112.6 %all-reduce.19.cloned.1.call-start = ((), (), s32[]{:S(2)}) async-start(), calls=%async_computation.3 | async-start | bytes 262144 | tf_op jit(solution)/shard_map/psum | solution.py:147
  52.2 118.5 %reduce-scatter.3.cloned.1.call-start = ((), (), s32[]{:S(2)}) async-start(), calls=%async_computation.4 | async-start | bytes 3932160 | tf_op jit(solution)/shard_map/reduce_scatter | solution.py:148
  133.3 37.4 %copy-start.12 = (f32[32,3,2,1024]{3,2,1,0:T(2,128)S(1)}, f32[32,3,2,1024]{3,2,1,0:T(2,128)}, u32[]{:S(2)}) copy-start(f32[32,3,2,1024]{3,2,1,0:T(2,128)} %param.6) | copy-start | bytes 2359300
  133.3 68.4 %all-gather.6.cloned.1.call-start = ((), (), s32[]{:S(2)}) async-start(), calls=%async_computation.5 | async-start | bytes 3932160 | tf_op jit(solution)/shard_map/all_gather | solution.py:146
  173.0 109.2 %all-reduce.21.cloned.1.call-start = ((), (), s32[]{:S(2)}) async-start(), calls=%async_computation.6 | async-start | bytes 262144 | tf_op jit(solution)/shard_map/psum | solution.py:147
  212.4 118.5 %reduce-scatter.5.cloned.1.call-start = ((), (), s32[]{:S(2)}) async-start(), calls=%async_computation.7 | async-start | bytes 3932160 | tf_op jit(solution)/shard_map/reduce_scatter | solution.py:148
  293.5 37.4 %copy-start.3 = (f32[32,3,2,1024]{3,0,2,1:T(8,128)S(1)}, f32[32,3,2,1024]{3,0,2,1:T(8,128)}, u32[]{:S(2)}) copy-start(f32[32,3,2,1024]{3,0,2,1:T(8,128)} %copy_subtract_fusion) | copy-start | bytes 2359300
  293.5 68.2 %all-gather.8.cloned.1.call-start = ((), (), s32[]{:S(2)}) async-start(), calls=%async_computation.8 | async-start | bytes 3932160 | tf_op jit(solution)/shard_map/all_gather | solution.py:152
  333.0 103.6 %all-reduce.23.cloned.1.call-start = ((), (), s32[]{:S(2)}) async-start(), calls=%async_computation.9 | async-start | bytes 131072 | tf_op jit(solution)/shard_map/psum | solution.py:155
  361.7 6.4 copy-start
  368.0 265.7 %all-reduce.25.cloned.1.call-start = ((), (), s32[]{:S(2)}) async-start(), calls=%async_computation.10 | async-start | bytes 786432 | tf_op jit(solution)/shard_map/psum | solution.py:176
  466.2 7.9 %copy-start.16 = (s32[2,1024]{1,0:T(2,128)S(1)}, s32[2,1024]{1,0:T(2,128)}, u32[]{:S(2)}) copy-start(s32[2,1024]{1,0:T(2,128)} %param.8) | copy-start | bytes 24580
  466.2 7.9 %copy-start.17 = (f32[8]{0:T(128)S(1)}, f32[8]{0:T(128)}, u32[]{:S(2)}) copy-start(f32[8]{0:T(128)} %param.9) | copy-start | bytes 100
  466.2 8.0 %copy-start.13 = (f32[256,128]{1,0:T(8,128)S(1)}, f32[256,128]{1,0:T(8,128)}, u32[]{:S(2)}) copy-start(f32[256,128]{1,0:T(8,128)} %all-reduce.19.cloned.1.call-done) | copy-start | bytes 393220
  466.2 8.0 %copy-start.14 = (f32[256,128]{1,0:T(8,128)S(1)}, f32[256,128]{1,0:T(8,128)}, u32[]{:S(2)}) copy-start(f32[256,128]{1,0:T(8,128)} %all-reduce.21.cloned.1.call-done) | copy-start | bytes 393220
  466.2 9.6 %copy-start.15 = (f32[3,2,1024]{2,1,0:T(2,128)S(1)}, f32[3,2,1024]{2,1,0:T(2,128)}, u32[]{:S(2)}) copy-start(f32[3,2,1024]{2,1,0:T(2,128)} %param.7) | copy-start | bytes 73732
  468.1 69.1 %collective-permute-start = (f32[128,3,1,1024]{3,0,2,1:T(8,128)}, f32[128,3,1,1024]{3,0,2,1:T(8,128)}, u32[]{:S(2)}, u32[]{:S(2)}) collective-permute-start(f32[128,3,1,1024]{3,0,2,1:T(8,128)} %get-tuple-element.21), channel_id=1, source_target_pairs={{0,4},{4,8},{8,12},{12,16},{16,20},{20,24},{24,28},{1,5},{5,9},{9,... | collective-permute-start | bytes 4718600 | tf_op jit(solution)/shard_map/ppermute | solution.py:17
  472.6 64.6 %collective-permute-start.1 = (f32[128,3,1,1024]{3,0,2,1:T(8,128)}, f32[128,3,1,1024]{3,0,2,1:T(8,128)}, u32[]{:S(2)}, u32[]{:S(2)}) collective-permute-start(f32[128,3,1,1024]{3,0,2,1:T(8,128)} %get-tuple-element.22), channel_id=1, source_target_pairs={{4,0},{8,4},{12,8},{16,12},{20,16},{24,20},{28,24},{5,1},{9,5},{13... | collective-permute-start | bytes 4718600 | tf_op jit(solution)/shard_map/ppermute | solution.py:18
  475.8 13.0 %slice-start = ((s8[6291456]{0:T(1024)(128)(4,1)}), s8[4194304]{0:T(1024)(128)(4,1)S(1)}, s32[]{:S(2)}) async-start(s8[6291456]{0:T(1024)(128)(4,1)} %bitcast.108), calls=%async_computation.11 | async-start | bytes 8388608
  479.0 9.9 %slice-start.1 = ((s8[6291456]{0:T(1024)(128)(4,1)}), s8[2097152]{0:T(1024)(128)(4,1)S(1)}, s32[]{:S(2)}) async-start(s8[6291456]{0:T(1024)(128)(4,1)} %bitcast.108), calls=%async_computation.12 | async-start | bytes 4194304
  553.0 7.3 %copy-start.9 = (f32[128,1,2,1024]{3,0,2,1:T(8,128)}, f32[128,1,2,1024]{3,0,2,1:T(8,128)S(1)}, u32[]{:S(2)}) copy-start(f32[128,1,2,1024]{3,0,2,1:T(8,128)S(1)} %add_bitcast_fusion) | copy-start | bytes 3145732
  561.1 6.0 copy-start.5
  561.1 6.0 copy-start.7
  (7 other events, 19.8 us)
Sparse Core Ops, SparseCore 0:
  10.1 31.2 all-gather.3
  52.3 69.6 all-reduce.18
  133.4 37.2 reduce-scatter.2
  173.1 28.5 all-gather.5
  212.5 69.6 all-reduce.20
  293.6 37.2 reduce-scatter.4
  333.1 28.5 all-gather.7
  368.1 68.4 all-reduce.22
  561.2 72.4 all-reduce.24
where the time goes:
time: 652 us; the launch traced here: 643 us
  waiting for transfers between devices  421 us (65%)
  matrix products  90.2 us (14%)
  other arithmetic  38.7 us (6%)
  blocking collectives  37.2 us (6%)
  local copies, waits for them, and re-layouts  34 us (5%)
  between operations  14.7 us (2%)
  starting transfers between devices  6.98 us (1%)
    psum x2, waiting for transfers between devices, shards(): coef_part = lax.psum(partial_value, 'grid')  124 us
    reduce_scatter x2, waiting for transfers between devices, shards(): lax.psum_scatter(combine_rows(coef_part, basis), 'cols', scatter_dimensio...  74.4 us
    psum x1, waiting for transfers between devices, shards(): gram_sum = lax.psum(cells_dot(finished, finished) / unknowns, 'grid')  66.2 us
    dot_general x9, matrix products, cells_dot(): lax.dot_general(left_flat, right_flat, (((1,), (1,)), ((), ())), precisio...  62.8 us
    all_gather x2, waiting for transfers between devices, shards(): lax.all_gather(current, 'cols', axis=0, tiled=True)  60.5 us
    ppermute x1, waiting for transfers between devices, padded(): before = lax.ppermute(last, axis, up)  41 us
    psum x1, blocking collectives, shards(): cross_terms, block_terms = lax.psum((cross_part, block_part), 'grid')  37.2 us
    all_gather x1, waiting for transfers between devices, shards(): finished = lax.all_gather(current, 'cols', axis=0, tiled=True)  28.2 us
  transfers between devices with their start and end apart: 11, of which 10 were waited for; matrix products, arithmetic and copies ran while one was open for 7% of the time, Pallas kernels for 0%

commit v1 on v0

--- a/solution.py
+++ b/solution.py
@@ -5,6 +5,27 @@
 
 NY = 32
 HIGHEST = lax.Precision.HIGHEST
+
+
+def ring_gather(array, axis, dim):
+    peers, mine, rows = (lax.axis_size(axis), lax.axis_index(axis), array.shape[dim])
+    right = [(i, (i + 1) % peers) for i in range(peers)]
+    left = [(i, (i - 1) % peers) for i in range(peers)]
+    out = jnp.zeros((*array.shape[:dim], peers * rows, *array.shape[dim + 1 :]), array.dtype)
+    out = lax.dynamic_update_slice_in_dim(out, array, mine * rows, axis=dim)
+    from_left = from_right = array
+    half = peers // 2
+    for turn in range(1, half + 1):
+        from_left = lax.ppermute(from_left, axis, right)
+        out = lax.dynamic_update_slice_in_dim(
+            out, from_left, (mine - turn) % peers * rows, axis=dim
+        )
+        if turn < peers - half:
+            from_right = lax.ppermute(from_right, axis, left)
+            out = lax.dynamic_update_slice_in_dim(
+                out, from_right, (mine + turn) % peers * rows, axis=dim
+            )
+    return out
 
 
 def padded(shard, sides, width):
@@ -149,7 +170,7 @@
             combine_rows(coef_part, basis), "cols", scatter_dimension=0, tiled=True
         )
         coefficients = coefficients + coef_part
-    finished = lax.all_gather(current, "cols", axis=0, tiled=True)
+    finished = ring_gather(current, "cols", 0)
     own_start = lax.axis_index("cols") * snap_cols
     identity = jnp.eye(total_snap, dtype=jnp.float32)
     gram_sum = lax.psum(cells_dot(finished, finished) / unknowns, "grid")

time: 652 us -> 753 us (1.15)
  local copies, waits for them, and re-layouts: 34 us -> 142 us
    dynamic_update_slice x0 -> x4, local copies, waits for them, and re-layouts: none -> 99.9 us  [the longest x2 51.2 us: ring_gather(): lax.dynamic_update_slice_in_dim(out, from_left, (mine - turn) % peers * r...]
    all_gather x1 -> x0, waiting for transfers between devices: 28.2 us -> none  [shards(): finished = lax.all_gather(current, 'cols', axis=0, tiled=True)]
    ppermute x0 -> x3, waiting for transfers between devices: none -> 17.9 us  [the longest x2 17.8 us: ring_gather(): from_left = lax.ppermute(from_left, axis, right)]
    ppermute x0 -> x3, local copies, waits for them, and re-layouts: none -> 9.36 us  [the longest x2 6.24 us: ring_gather(): from_left = lax.ppermute(from_left, axis, right)]
  transfers between devices with their start and end apart: 11 -> 13, of which waited for: 10 -> 10; matrix products, arithmetic and copies ran while one was open for 7% -> 17% of each run, Pallas kernels for 0% -> 0%
where the time goes in v1:
time: 753 us; the launch traced here: 743 us
  waiting for transfers between devices  417 us (55%)
  local copies, waits for them, and re-layouts  142 us (19%)
  matrix products  86.9 us (12%)
  blocking collectives  37.2 us (5%)
  other arithmetic  36.7 us (5%)
  between operations  14.9 us (2%)
  starting transfers between devices  8.18 us (1%)
    psum x2, waiting for transfers between devices, shards(): coef_part = lax.psum(partial_value, 'grid')  124 us
    reduce_scatter x2, waiting for transfers between devices, shards(): lax.psum_scatter(combine_rows(coef_part, basis), 'cols', scatter_dimensio...  74.2 us
    psum x1, waiting for transfers between devices, shards(): gram_sum = lax.psum(cells_dot(finished, finished) / unknowns, 'grid')  69.2 us
    all_gather x2, waiting for transfers between devices, shards(): lax.all_gather(current, 'cols', axis=0, tiled=True)  60.5 us
    dot_general x9, matrix products, cells_dot(): lax.dot_general(left_flat, right_flat, (((1,), (1,)), ((), ())), precisio...  59.4 us
    dynamic_update_slice x2, local copies, waits for them, and re-layouts, ring_gather(): lax.dynamic_update_slice_in_dim(out, from_left, (mine - turn) % peers * r...  51.2 us
    ppermute x1, waiting for transfers between devices, padded(): before = lax.ppermute(last, axis, up)  45.3 us
    psum x1, blocking collectives, shards(): cross_terms, block_terms = lax.psum((cross_part, block_part), 'grid')  37.2 us
  transfers between devices with their start and end apart: 13, of which 10 were waited for; matrix products, arithmetic and copies ran while one was open for 17% of the time, Pallas kernels for 0%

profile of v1, /device:TPU:0, one launch (start us, length us, event | category | flops | bytes accessed | tf_op | source)
XLA Modules:
  0.0 743.1 jit_solution(14907837654088508062)
XLA Ops:
  9.5 31.9 %all-gather.3.cloned.1.call-done = f32[128,3,2,1024]{3,0,2,1:T(8,128)} async-done(((f32[32,3,2,1024]{3,0,2,1:T(8,128)}), f32[128,3,2,1024]{3,0,2,1:T(8,128)}) %all-gather.3.cloned.1.call-update) | async-done | bytes 3145744 | tf_op jit(solution)/shard_map/all_gather | solution.py:167
  41.4 10.8 %fusion.23 = f32[256,128]{1,0:T(8,128)} fusion(f32[128,3,2,1024]{3,0,2,1:T(8,128)} %all-gather.3.cloned.1.call-done, f32[256,3,2,1024]{3,2,1,0:T(2,128)} %param.5), kind=kOutput, calls=%fused_computation.28 | convolution fusion | flops 2415919104 | bytes 9568256 | tf_op jit(solution)/shard_map/dot_general | solution.py:47
  52.2 9.0 %reshape.49 = f32[256,6144]{1,0:T(8,128)} reshape(f32[256,3,2,1024]{3,2,1,0:T(2,128)} %param.5) | data formatting | bytes 12582912 | tf_op jit(solution)/shard_map/reshape | solution.py:45
  67.8 54.2 %all-reduce.19.cloned.1.call-done = f32[256,128]{1,0:T(8,128)} async-done(((f32[256,128]{1,0:T(8,128)}), f32[256,128]{1,0:T(8,128)}) %all-reduce.19.cloned.1.call-update) | async-done | bytes 131088 | tf_op jit(solution)/shard_map/psum | solution.py:168
  122.0 11.2 %fusion.63 = f32[128,3,2,1024]{3,0,2,1:T(8,128)} fusion(f32[3,2,1024,256]{3,2,1,0:T(8,128)} %bitcast.110, f32[256,128]{1,0:T(8,128)} %all-reduce.19.cloned.1.call-done), kind=kOutput, calls=%fused_computation.61 | convolution fusion | flops 2415919104 | bytes 9568256 | tf_op jit(solution)/shard_map/dot_general | solution.py:58
  133.8 36.9 %reduce-scatter.3.cloned.1.call-done = f32[32,3,2,1024]{3,0,2,1:T(8,128)} async-done(((f32[128,3,2,1024]{3,0,2,1:T(8,128)}), f32[32,3,2,1024]{3,0,2,1:T(8,128)}) %reduce-scatter.3.cloned.1.call-update) | async-done | bytes 786448 | tf_op jit(solution)/shard_map/reduce_scatter | solution.py:169
  173.1 28.6 %all-gather.5.cloned.1.call-done = f32[128,3,2,1024]{3,0,2,1:T(8,128)} async-done(((f32[32,3,2,1024]{3,0,2,1:T(8,128)}), f32[128,3,2,1024]{3,0,2,1:T(8,128)}) %all-gather.5.cloned.1.call-update) | async-done | bytes 3145744 | tf_op jit(solution)/shard_map/all_gather | solution.py:167
  201.7 10.7 %fusion.26 = f32[256,128]{1,0:T(8,128)} fusion(f32[128,3,2,1024]{3,0,2,1:T(8,128)} %all-gather.5.cloned.1.call-done, f32[256,3,2,1024]{3,2,1,0:T(2,128)} %param.5), kind=kOutput, calls=%fused_computation.29 | convolution fusion | flops 2415919104 | bytes 9568256 | tf_op jit(solution)/shard_map/dot_general | solution.py:47
  212.4 69.8 %all-reduce.21.cloned.1.call-done = f32[256,128]{1,0:T(8,128)} async-done(((f32[256,128]{1,0:T(8,128)}), f32[256,128]{1,0:T(8,128)}) %all-reduce.21.cloned.1.call-update) | async-done | bytes 131088 | tf_op jit(solution)/shard_map/psum | solution.py:168
  282.2 11.2 %fusion.61 = f32[128,3,2,1024]{3,0,2,1:T(8,128)} fusion(f32[3,2,1024,256]{3,2,1,0:T(8,128)} %bitcast.111, f32[256,128]{1,0:T(8,128)} %all-reduce.21.cloned.1.call-done), kind=kOutput, calls=%fused_computation.59 | convolution fusion | flops 2415919104 | bytes 9568256 | tf_op jit(solution)/shard_map/dot_general | solution.py:58
  293.5 37.3 %reduce-scatter.5.cloned.1.call-done = f32[32,3,2,1024]{3,0,2,1:T(8,128)} async-done(((f32[128,3,2,1024]{3,0,2,1:T(8,128)}), f32[32,3,2,1024]{3,0,2,1:T(8,128)}) %reduce-scatter.5.cloned.1.call-update) | async-done | bytes 786448 | tf_op jit(solution)/shard_map/reduce_scatter | solution.py:169
  334.7 17.8 %collective-permute-done = f32[32,3,2,1024]{3,0,2,1:T(8,128)} collective-permute-done((f32[32,3,2,1024]{3,0,2,1:T(8,128)}, f32[32,3,2,1024]{3,0,2,1:T(8,128)}, u32[]{:S(2)}, u32[]{:S(2)}) %collective-permute-start) | collective-permute-done | bytes 786464 | tf_op jit(solution)/shard_map/ppermute | solution.py:19
  356.1 23.0 %dynamic_update_slice.12 = f32[128,3,2,1024]{0,3,2,1:T(8,128)S(1)} dynamic-update-slice(f32[128,3,2,1024]{0,3,2,1:T(8,128)S(1)} %broadcast_in_dim.58, f32[32,3,2,1024]{0,3,2,1:T(8,128)} %copy.53, s32[]{:T(128)S(6)} %select_n.94, s32[]{:T(128)} %constant.117.clone.1, s32[]{:T(128)} %constant.117.clone.1, s32[]{:T(128)} %constant.117.clone.1) | dynamic-update-slice | bytes 1572868 | tf_op jit(solution)/shard_map/dynamic_update_slice | solution.py:15
  382.3 25.6 %dynamic_update_slice.13 = f32[128,3,2,1024]{0,3,2,1:T(8,128)S(1)} dynamic-update-slice(f32[128,3,2,1024]{0,3,2,1:T(8,128)S(1)} %dynamic_update_slice.12, f32[32,3,2,1024]{0,3,2,1:T(8,128)} %copy.54, s32[]{:T(128)S(6)} %select_n.96, s32[]{:T(128)} %constant.117.clone.1, s32[]{:T(128)} %constant.117.clone.1, s32[]{:T(128)} %constant.117.clone.1) | dynamic-update-slice | bytes 1572868 | tf_op jit(solution)/shard_map/dynamic_update_slice | solution.py:20
  411.1 25.6 %dynamic_update_slice.14 = f32[128,3,2,1024]{0,3,2,1:T(8,128)S(1)} dynamic-update-slice(f32[128,3,2,1024]{0,3,2,1:T(8,128)S(1)} %dynamic_update_slice.13, f32[32,3,2,1024]{0,3,2,1:T(8,128)} %copy.55, s32[]{:T(128)S(6)} %select_n.98, s32[]{:T(128)} %constant.117.clone.1, s32[]{:T(128)} %constant.117.clone.1, s32[]{:T(128)} %constant.117.clone.1) | dynamic-update-slice | bytes 1572868 | tf_op jit(solution)/shard_map/dynamic_update_slice | solution.py:25
  439.8 25.6 %dynamic_update_slice.15 = f32[128,3,2,1024]{0,3,2,1:T(8,128)S(1)} dynamic-update-slice(f32[128,3,2,1024]{0,3,2,1:T(8,128)S(1)} %dynamic_update_slice.14, f32[32,3,2,1024]{0,3,2,1:T(8,128)} %copy.56, s32[]{:T(128)S(6)} %select_n.100, s32[]{:T(128)} %constant.117.clone.1, s32[]{:T(128)} %constant.117.clone.1, s32[]{:T(128)} %constant.117.clone.1) | dynamic-update-slice | bytes 1572868 | tf_op jit(solution)/shard_map/dynamic_update_slice | solution.py:20
  471.5 69.2 %all-reduce.23.cloned.1.call-done = f32[128,128]{0,1:T(8,128)} async-done(((f32[128,128]{0,1:T(8,128)}), f32[128,128]{0,1:T(8,128)}) %all-reduce.23.cloned.1.call-update) | async-done | bytes 65552 | tf_op jit(solution)/shard_map/psum | solution.py:176
  542.5 11.7 %cholesky.17 = f32[128,128]{1,0:T(8,128)S(1)} custom-call(f32[128,128]{1,0:T(8,128)S(1)} %fusion.67), custom_call_target="Cholesky" | custom-call | tf_op jit(solution)/shard_map/jit(cholesky)/cholesky | solution.py:177
  555.5 9.8 %custom-call.7 = f32[1,128,128]{1,2,0:T(8,128)S(1)} custom-call(f32[1,128,128]{2,1,0:T(8,128)S(1)} %fusion.65), custom_call_target="InvertDiagBlocksLowerTriangular" | custom-call | tf_op jit(solution)/shard_map/jit(_solve_triangular)/triangular_solve | solution.py:178
  587.2 7.2 fusion.32
  594.4 45.3 %collective-permute-done.3 = f32[128,3,1,1024]{3,0,2,1:T(8,128)S(1)} collective-permute-done((f32[128,3,1,1024]{3,0,2,1:T(8,128)S(1)}, f32[128,3,1,1024]{3,0,2,1:T(8,128)S(1)}, u32[]{:S(2)}, u32[]{:S(2)}) %collective-permute-start.3) | collective-permute-done | bytes 1572896 | tf_op jit(solution)/shard_map/ppermute | solution.py:38
  653.4 7.2 fusion.29
  670.7 37.2 %psum.39 = f32[3,32,128]{2,1,0:T(8,128)} all-reduce(f32[3,32,128]{2,1,0:T(8,128)S(1)} %maximum_multiply_fusion), channel_id=1, replica_groups=mesh['grid'=8,'cols'=4] {'grid'}, use_global_device_ids=true, to_apply=%region_9.10 | all-reduce | flops 12288 | bytes 98304 | tf_op jit(solution)/shard_map/psum | solution.py:197
  707.9 26.2 %all-reduce.25.cloned.1.call-done = f32[3,256,128]{1,2,0:T(8,128)} async-done(((f32[3,256,128]{1,2,0:T(8,128)}), f32[3,256,128]{1,2,0:T(8,128)}) %all-reduce.25.cloned.1.call-update) | async-done | bytes 393232 | tf_op jit(solution)/shard_map/psum | solution.py:197
  (103 shorter events, 84.9 us)
Async XLA Ops:
  7.2 34.2 %all-gather.3.cloned.1.call-start = ((), (), s32[]{:S(2)}) async-start(), calls=%async_computation.2 | async-start | bytes 3932160 | tf_op jit(solution)/shard_map/all_gather | solution.py:167
  9.5 112.6 %all-reduce.19.cloned.1.call-start = ((), (), s32[]{:S(2)}) async-start(), calls=%async_computation.3 | async-start | bytes 262144 | tf_op jit(solution)/shard_map/psum | solution.py:168
  52.2 118.5 %reduce-scatter.3.cloned.1.call-start = ((), (), s32[]{:S(2)}) async-start(), calls=%async_computation.4 | async-start | bytes 3932160 | tf_op jit(solution)/shard_map/reduce_scatter | solution.py:169
  133.3 37.4 %copy-start.12 = (f32[32,3,2,1024]{3,2,1,0:T(2,128)S(1)}, f32[32,3,2,1024]{3,2,1,0:T(2,128)}, u32[]{:S(2)}) copy-start(f32[32,3,2,1024]{3,2,1,0:T(2,128)} %param.6) | copy-start | bytes 2359300
  133.3 68.4 %all-gather.5.cloned.1.call-start = ((), (), s32[]{:S(2)}) async-start(), calls=%async_computation.5 | async-start | bytes 3932160 | tf_op jit(solution)/shard_map/all_gather | solution.py:167
  173.0 109.2 %all-reduce.21.cloned.1.call-start = ((), (), s32[]{:S(2)}) async-start(), calls=%async_computation.6 | async-start | bytes 262144 | tf_op jit(solution)/shard_map/psum | solution.py:168
  212.4 118.5 %reduce-scatter.5.cloned.1.call-start = ((), (), s32[]{:S(2)}) async-start(), calls=%async_computation.7 | async-start | bytes 3932160 | tf_op jit(solution)/shard_map/reduce_scatter | solution.py:169
  293.5 37.4 %copy-start.3 = (f32[32,3,2,1024]{3,0,2,1:T(8,128)S(1)}, f32[32,3,2,1024]{3,0,2,1:T(8,128)}, u32[]{:S(2)}) copy-start(f32[32,3,2,1024]{3,0,2,1:T(8,128)} %copy_subtract_fusion) | copy-start | bytes 2359300
  293.5 247.2 %all-reduce.23.cloned.1.call-start = ((), (), s32[]{:S(2)}) async-start(), calls=%async_computation.8 | async-start | bytes 131072 | tf_op jit(solution)/shard_map/psum | solution.py:176
  333.0 19.6 %collective-permute-start = (f32[32,3,2,1024]{3,0,2,1:T(8,128)}, f32[32,3,2,1024]{3,0,2,1:T(8,128)}, u32[]{:S(2)}, u32[]{:S(2)}) collective-permute-start(f32[32,3,2,1024]{3,0,2,1:T(8,128)} %sub.82), channel_id=1, source_target_pairs={{0,1},{1,2},{2,3},{3,0},{4,5},{5,6},{6,7},{7,4},{8,9},{9,10},{10,1... | collective-permute-start | bytes 2359304 | tf_op jit(solution)/shard_map/ppermute | solution.py:19
  333.0 75.0 %collective-permute-start.1 = (f32[32,3,2,1024]{3,0,2,1:T(8,128)}, f32[32,3,2,1024]{3,0,2,1:T(8,128)}, u32[]{:S(2)}, u32[]{:S(2)}) collective-permute-start(f32[32,3,2,1024]{3,0,2,1:T(8,128)} %sub.82), channel_id=1, source_target_pairs={{0,3},{1,0},{2,1},{3,2},{4,7},{5,4},{6,5},{7,6},{8,11},{9,8},{10,9... | collective-permute-start | bytes 2359304 | tf_op jit(solution)/shard_map/ppermute | solution.py:24
  352.6 84.1 %collective-permute-start.2 = (f32[32,3,2,1024]{3,0,2,1:T(8,128)}, f32[32,3,2,1024]{3,0,2,1:T(8,128)}, u32[]{:S(2)}, u32[]{:S(2)}) collective-permute-start(f32[32,3,2,1024]{3,0,2,1:T(8,128)} %collective-permute-done), channel_id=1, source_target_pairs={{0,1},{1,2},{2,3},{3,0},{4,5},{5,6},{6,7},{7,4},{8,9},{9,10},{10,1... | collective-permute-start | bytes 2359304 | tf_op jit(solution)/shard_map/ppermute | solution.py:19
  465.4 5.7 copy-start
  471.2 262.9 %all-reduce.25.cloned.1.call-start = ((), (), s32[]{:S(2)}) async-start(), calls=%async_computation.9 | async-start | bytes 786432 | tf_op jit(solution)/shard_map/psum | solution.py:197
  565.6 14.5 %slice-start = ((s8[6291456]{0:T(1024)(128)(4,1)}), s8[4194304]{0:T(1024)(128)(4,1)S(1)}, s32[]{:S(2)}) async-start(s8[6291456]{0:T(1024)(128)(4,1)} %bitcast.108), calls=%async_computation.10 | async-start | bytes 8388608
  570.5 6.4 copy-start.15
  570.5 9.6 %slice-start.1 = ((s8[6291456]{0:T(1024)(128)(4,1)}), s8[2097152]{0:T(1024)(128)(4,1)S(1)}, s32[]{:S(2)}) async-start(s8[6291456]{0:T(1024)(128)(4,1)} %bitcast.108), calls=%async_computation.11 | async-start | bytes 4194304
  570.7 69.0 %collective-permute-start.3 = (f32[128,3,1,1024]{3,0,2,1:T(8,128)S(1)}, f32[128,3,1,1024]{3,0,2,1:T(8,128)S(1)}, u32[]{:S(2)}, u32[]{:S(2)}) collective-permute-start(f32[128,3,1,1024]{3,0,2,1:T(8,128)S(1)} %get-tuple-element.21), channel_id=1, source_target_pairs={{0,4},{4,8},{8,12},{12,16},{16,20},{20,24},{24,28},{1,5},{5,9},{9,... | collective-permute-start | bytes 4718600 | tf_op jit(solution)/shard_map/ppermute | solution.py:38
  574.3 65.4 %collective-permute-start.4 = (f32[128,3,1,1024]{3,0,2,1:T(8,128)S(1)}, f32[128,3,1,1024]{3,0,2,1:T(8,128)S(1)}, u32[]{:S(2)}, u32[]{:S(2)}) collective-permute-start(f32[128,3,1,1024]{3,0,2,1:T(8,128)S(1)} %get-tuple-element.22), channel_id=1, source_target_pairs={{4,0},{8,4},{12,8},{16,12},{20,16},{24,20},{28,24},{5,1},{9,5},{13... | collective-permute-start | bytes 4718600 | tf_op jit(solution)/shard_map/ppermute | solution.py:39
  576.9 10.3 %copy-start.1 = (f32[32,3,2,1024]{3,0,2,1:T(8,128)}, f32[32,3,2,1024]{3,0,2,1:T(8,128)S(1)}, u32[]{:S(2)}) copy-start(f32[32,3,2,1024]{3,0,2,1:T(8,128)S(1)} %constant_dynamic-slice_fusion) | copy-start | bytes 2359300
  653.4 7.3 copy-start.9
  661.5 6.0 copy-start.5
  661.5 6.0 copy-start.7
  661.5 6.0 copy-start.10
  (9 other events, 35.5 us)
Sparse Core Ops, SparseCore 0:
  10.1 31.2 all-gather.2
  52.3 69.6 all-reduce.18
  133.4 37.2 reduce-scatter.2
  173.1 28.5 all-gather.4
  212.5 69.6 all-reduce.20
  293.6 37.2 reduce-scatter.4
  471.3 69.3 all-reduce.22
  661.6 72.4 all-reduce.24
